TPU v7x, 128 devices: a whole 4x4x4 slice. The times are simulated.
128 devices in a mesh: aux: 4 (over y), occ: 32 (over z, x, core).
Axes of the slice: x: 4, y: 4, z: 4, core: 2. Of those that a mesh axis runs over, the one named last changes fastest.
Arguments:
- slab: bfloat16 [128, 8192, 512], P(None, ('aux', 'occ')), may hold values from -6 to 6
- domain_class: int32 [128], replicated, may hold values from 0 to 3
- pairs: int32 [512, 2], P('occ'), may hold values from 0 to 127, as said below
Outputs:
- exchange_ints: bfloat16 [512, 512, 512], P('occ', 'aux')
Inputs may be any that keep to these rules, and one draw needn't show every extreme that they name: `pairs`: pair row p belongs to occ index o = p // 16; its first orbital lies in [o * 4, (o + 1) * 4) and its second in [o * 4, min((o + 2) * 4, 128)).
All inputs are finite; a program needn't handle non-finite values.
Results may differ from a plain program's by a relative error of at most 0.0012.
Values may be sent and summed in bfloat16 or wider, within the bound.
A program may use at most 128 MiB of HBM per device.

v0:
```python
import jax
import jax.numpy as jnp
from jax import lax
from jax.sharding import PartitionSpec as P

DOM = 512
SLAB = 8192
OCC_DEV = 4


def passed_along(shard, axis, by):
    count = lax.axis_size(axis)
    pairs = [(i, i + by) for i in range(count) if 0 <= i + by < count]
    return lax.ppermute(shard, axis, pairs)


def on_device(slab, domain_class, pairs):
    shard = lax.axis_index("occ")
    start = shard * OCC_DEV
    mine = lax.all_to_all(slab, "occ", split_axis=0, concat_axis=1, tiled=True)
    ahead = passed_along(mine, "occ", -1)
    blocks = jnp.concatenate([mine, ahead], axis=0)
    padded_class = jnp.concatenate([domain_class, jnp.zeros((2 * OCC_DEV,), jnp.int32)])
    classes = lax.dynamic_slice_in_dim(padded_class, start, 2 * OCC_DEV)
    size = (classes + 1) * (DOM // 4)
    mask = jnp.arange(DOM, dtype=jnp.int32)[None, :] < size[:, None]
    blocks = jnp.where(mask[:, None, :], blocks, jnp.zeros_like(blocks))
    factor = 1.0 / jnp.sqrt(jnp.float32(SLAB))
    local_pairs = pairs - start

    def one_pair(pair):
        left = lax.dynamic_index_in_dim(blocks, pair[0], 0, keepdims=False)
        right = lax.dynamic_index_in_dim(blocks, pair[1], 0, keepdims=False)
        total = lax.dot_general(
            left, right, (((0,), (0,)), ((), ())), preferred_element_type=jnp.float32
        )
        return total * factor

    partial_value = lax.map(one_pair, local_pairs)
    summed = lax.psum_scatter(partial_value, "aux", scatter_dimension=1, tiled=True)
    return summed.astype(jnp.bfloat16)


def solution(mesh):
    in_specs = (P(None, ("aux", "occ"), None), P(), P("occ", None))
    out_specs = P("occ", "aux", None)
    return jax.shard_map(
        on_device, mesh=mesh, in_specs=in_specs, out_specs=out_specs, check_vma=False
    )
```

profile of v0, /device:TPU:97, one launch (start us, length us, event | category | flops | bytes accessed | tf_op | source)
XLA Modules:
  0.0 522.3 jit_solution(423762808345827316)
XLA Ops:
  6.5 101.1 %all_to_all.18 = bf16[128,64,512]{2,1,0:T(8,128)(2,1)} all-to-all(bf16[128,64,512]{2,1,0:T(8,128)(2,1)} %param.5), channel_id=1, replica_groups=mesh['aux'=4,'occ'=32] {'occ'}, dimensions={0} | all-to-all | bytes 16777216 | tf_op jit(solution)/shard_map/all_to_all | solution.py:20
  107.7 7.7 %copy.4 = bf16[32,4,64,512]{3,2,0,1:T(8,128)(2,1)} copy(bf16[32,4,64,512]{3,2,1,0:T(8,128)(2,1)} %bitcast.30) | data formatting | bytes 16777216 | tf_op jit(solution)/shard_map/all_to_all | solution.py:20
  115.4 2.7 collective-permute-start
  118.2 92.2 %collective-permute-done = bf16[4,2048,512]{2,1,0:T(8,128)(2,1)} collective-permute-done((bf16[4,2048,512]{2,1,0:T(8,128)(2,1)}, bf16[4,2048,512]{2,1,0:T(8,128)(2,1)}, u32[]{:S(2)}, u32[]{:S(2)}) %collective-permute-start) | collective-permute-done | bytes 8388640 | tf_op jit(solution)/shard_map/ppermute | solution.py:14
  210.4 14.2 %maximum_select_fusion = bf16[8,2048,512]{2,1,0:T(8,128)(2,1)} fusion(bf16[4,2048,512]{2,1,0:T(8,128)(2,1)} %collective-permute-done, bf16[4,2048,512]{2,1,0:T(8,128)(2,1)} %bitcast.29, pred[8,512]{1,0:T(8,128)(4,1)S(1)} %iota_compare_fusion), kind=kLoop, calls=%fused_computation.8 | loop fusion | flops 16777216 | bytes 33558528 | tf_op jit(solution)/shard_map/jit(_where)/select_n | solution.py:27
  224.7 137.3 %while.10 = (s32[]{:T(128)}, f32[16,512,512]{2,1,0:T(8,128)}, s32[16,2]{0,1:T(2,128)S(1)}, bf16[8,2048,512]{2,1,0:T(8,128)(2,1)}, s32[]{:T(128)}, /*index=5*/s32[]{:T(128)}, s32[]{:T(128)}) while((s32[]{:T(128)}, f32[16,512,512]{2,1,0:T(8,128)}, s32[16,2]{0,1:T(2,128)S(1)}, bf16[8,2048,512]{2,1,0:T(8,128)(2,1)}, s32[]{:T(128)}, ...), condition=%wide.region_1.2_spmd, body=%wide.region_0.1_spmd.sunk | while | flops 1074003968 | bytes 5243581 | solution.py:39
  224.7 0.5 fusion.18
  228.7 4.5 bitcast_dynamic-update-slice_fusion.2
  237.3 4.5 bitcast_dynamic-update-slice_fusion.2
  245.9 4.5 bitcast_dynamic-update-slice_fusion.2
  250.5 0.5 fusion.18
  254.5 4.5 bitcast_dynamic-update-slice_fusion.2
  259.1 0.5 fusion.18
  263.1 4.5 bitcast_dynamic-update-slice_fusion.2
  271.6 4.5 bitcast_dynamic-update-slice_fusion.2
  276.2 0.5 fusion.18
  280.2 4.5 bitcast_dynamic-update-slice_fusion.2
  288.8 4.5 bitcast_dynamic-update-slice_fusion.2
  293.4 0.5 fusion.18
  297.4 4.5 bitcast_dynamic-update-slice_fusion.2
  306.0 4.5 bitcast_dynamic-update-slice_fusion.2
  310.6 0.5 fusion.18
  314.6 4.5 bitcast_dynamic-update-slice_fusion.2
  323.1 4.5 bitcast_dynamic-update-slice_fusion.2
  331.7 4.5 bitcast_dynamic-update-slice_fusion.2
  336.3 0.5 fusion.18
  340.3 4.5 bitcast_dynamic-update-slice_fusion.2
  344.9 0.5 fusion.18
  348.9 4.5 bitcast_dynamic-update-slice_fusion.2
  357.5 4.5 bitcast_dynamic-update-slice_fusion.2
  362.0 149.7 %reduce-scatter.2.cloned.1.call-done = f32[16,128,512]{2,1,0:T(8,128)} async-done(((f32[16,512,512]{2,1,0:T(8,128)}), f32[16,128,512]{2,1,0:T(8,128)}) %reduce-scatter.2.cloned.1.call-update) | async-done | bytes 4194320 | tf_op jit(solution)/shard_map/reduce_scatter | solution.py:40
  511.7 3.8 convert_element_type.3
  (34 shorter events, 5.5 us)
Async XLA Ops:
  6.5 111.5 %copy-start.1 = (s32[128]{0:T(128)S(1)}, s32[128]{0:T(128)}, u32[]{:S(2)}) copy-start(s32[128]{0:T(128)} %param.6) | copy-start | bytes 1540
  6.5 111.6 %copy-start = (s32[16,2]{0,1:T(2,128)S(1)}, s32[16,2]{0,1:T(2,128)}, u32[]{:S(2)}) copy-start(s32[16,2]{0,1:T(2,128)} %param.7) | copy-start | bytes 388
  6.5 505.2 %reduce-scatter.2.cloned.1.call-start = ((), (), s32[]{:S(2)}) async-start(), calls=%async_computation.2 | async-start | bytes 20971520 | tf_op jit(solution)/shard_map/reduce_scatter | solution.py:40
  115.4 95.1 %collective-permute-start = (bf16[4,2048,512]{2,1,0:T(8,128)(2,1)}, bf16[4,2048,512]{2,1,0:T(8,128)(2,1)}, u32[]{:S(2)}, u32[]{:S(2)}) collective-permute-start(bf16[4,2048,512]{2,1,0:T(8,128)(2,1)} %bitcast.28), channel_id=1, source_target_pairs={{1,0},{2,1},{3,2},{4,3},{5,4},{6,5},{7,6},{8,7},{9,8},{10,9},{11,1... | collective-permute-start | bytes 25165832 | tf_op jit(solution)/shard_map/ppermute | solution.py:14
Sparse Core Ops, SparseCore 0:
  362.1 149.5 reduce-scatter.1
where the time goes:
time: 525 us; the launch traced here: 522 us
  waiting for transfers between devices  242 us (46%)
  blocking collectives  101 us (19%)
  matrix products  72 us (14%)
  loops' own time  55.8 us (11%)
  other arithmetic  18.2 us (3%)
  local copies, waits for them, and re-layouts  17.3 us (3%)
  between operations  13.4 us (3%)
    reduce_scatter x1, waiting for transfers between devices, on_device(): lax.psum_scatter(partial_value, 'aux', scatter_dimension=1, tiled=True)  150 us
    all_to_all x1, blocking collectives, on_device(): mine = lax.all_to_all(slab, 'occ', split_axis=0, concat_axis=1, tiled=True)  101 us
    ppermute x1, waiting for transfers between devices, passed_along(): return lax.ppermute(shard, axis, pairs)  92.2 us
    dot_general x16, matrix products, one_pair(): lax.dot_general(left, right, (((0,), (0,)), ((), ())), preferred_element_...  72 us
    another operation x1, loops' own time, on_device(): partial_value = lax.map(one_pair, local_pairs)  55.8 us
    select_n x1, other arithmetic, on_device(): blocks = jnp.where(mask[:, None, :], blocks, jnp.zeros_like(blocks))  14.2 us
  transfers between devices with their start and end apart: 2, of which 2 were waited for; matrix products, arithmetic and copies ran while one was open for 0% of the time, Pallas kernels for 0%

commit v1 on v0

v1 whole, which is shorter than its diff:
```python
import functools

import jax
import jax.numpy as jnp
from jax import lax
from jax.experimental import pallas as pl
from jax.experimental.pallas import tpu as pltpu
from jax.sharding import PartitionSpec as P

DOM = 512
SLAB = 8192
OCC_DEV = 4
PAIRS_DEV = 16
N_AUX = 4
SIDE = 4
CHIPS = SIDE * SIDE
N_OCC = 2 * CHIPS
ROWS = 64
KLOC = N_OCC * ROWS
HALF = KLOC // 2
COL = DOM // 4
GROUP = 4
NOCC = N_OCC * OCC_DEV
MESH = pl.DeviceIdType.MESH
LEVELS = 32767.0
TINY = 1e-33
BF16 = jnp.bfloat16


def kernel(classes, pairs, slab, out, *scratch):
    cols = scratch[:4]
    (left, total, outbox, inbox, outscale, inscale,
     got, sent, own_sem, mid_got, mid_sent, part_got, part_sent, scale_got, scale_sent) = scratch[4:]
    a = lax.axis_index("aux")
    o = lax.axis_index("occ")
    chip = o // 2
    core = lax.rem(o, 2)
    z, x = chip // SIDE, lax.rem(chip, SIDE)
    start = o * OCC_DEV
    sibling = o + 1 - 2 * core
    mine = pl.ds(core * HALF + chip * ROWS, ROWS)

    barrier = pltpu.get_barrier_semaphore()

    def greet_occ(s, carry):
        pl.semaphore_signal(barrier, inc=1, device_id=(a, lax.rem(o + s, N_OCC)), device_id_type=MESH)
        return carry

    def greet_aux(s, carry):
        pl.semaphore_signal(barrier, inc=1, device_id=(lax.rem(a + s, N_AUX), o), device_id_type=MESH)
        return carry

    lax.fori_loop(1, N_OCC, greet_occ, 0)
    lax.fori_loop(1, N_AUX, greet_aux, 0)

    def column(q):
        return pl.ds(pl.multiple_of(lax.rem(a + q + 1, 4) * COL, COL), COL)

    def own_copy(q, orbital, count, slot):
        return pltpu.make_async_copy(
            slab.at[pl.ds(orbital, count), :, column(q)], cols[q].at[pl.ds(slot, count), mine, :], own_sem.at[q]
        )

    def slab_copy(q, to_chip, to_core, orbital, count, slot):
        return pltpu.make_async_remote_copy(
            src_ref=slab.at[pl.ds(orbital, count), :, column(q)],
            dst_ref=cols[q].at[pl.ds(slot, count), mine, :],
            send_sem=sent.at[q],
            recv_sem=got.at[q],
            device_id=(a, 2 * to_chip + to_core),
            device_id_type=MESH,
        )

    for q in range(4):
        own_copy(q, start, OCC_DEV, 0).start()

        @pl.when(core == 0)
        def _():
            own_copy(q, start + OCC_DEV, OCC_DEV, OCC_DEV).start()

    pl.semaphore_wait(barrier, N_OCC - 1 + N_AUX - 1)

    def send_columns(q):
        ahead = lax.rem(8 * chip + 8, NOCC)

        @pl.when(core == 0)
        def _():
            slab_copy(q, chip, 1, ahead, 4, 4).start()

        @pl.when(core == 1)
        def _():
            slab_copy(q, chip, 0, 8 * chip, 4, 0).start()
            own_copy(q, ahead, 4, 4).start()

        def body(s, carry):
            step = lax.rem(7 * s, CHIPS)
            step = step + core * (CHIPS - 2 * step)
            to = lax.rem(z + step // SIDE, SIDE) * SIDE + lax.rem(x + lax.rem(step, SIDE), SIDE)
            base = 8 * to
            beyond = lax.rem(base + 8, NOCC)

            @pl.when(core == 0)
            def _():
                slab_copy(q, to, 0, base, 8, 0).start()
                slab_copy(q, to, 1, beyond, 4, 4).start()

            @pl.when(core == 1)
            def _():
                slab_copy(q, to, 0, base, 4, 0).start()
                slab_copy(q, to, 1, base + 4, 4, 0).start()
                slab_copy(q, to, 1, beyond, 4, 4).start()

            return carry

        lax.fori_loop(1, CHIPS, body, 0)

    for q in range(4):
        send_columns(q)

    def wait_bytes(ref, sem):
        pltpu.make_async_copy(ref, ref, sem).wait()

    def remote_part(q):
        return cols[q].at[:, pl.ds(0, 23 * ROWS), :]

    def middle_copy(q):
        half = pl.ds(core * HALF, HALF)
        return pltpu.make_async_remote_copy(
            src_ref=cols[q].at[pl.ds(4 - 4 * core, 4), half, :],
            dst_ref=cols[q].at[pl.ds(4 * core, 4), half, :],
            send_sem=mid_sent.at[q],
            recv_sem=mid_got.at[q],
            device_id=(a, sibling),
            device_id_type=MESH,
        )

    def arrive(q):
        wait_bytes(cols[q].at[:, pl.ds(0, ROWS), :], own_sem.at[q])
        wait_bytes(remote_part(q), got.at[q])
        middle_copy(q).start()

    def settle(q):
        middle_copy(q).wait()
        for i in range(OCC_DEV):
            left[i, q * COL:(q + 1) * COL, :] = cols[q][i].T

    factor = 1.0 / jnp.sqrt(jnp.float32(SLAB))

    def weight(p, m, n):
        keep_m = lax.rem(a + m + 1, 4) <= classes[pairs[p, 0]]
        keep_n = lax.rem(a + n + 1, 4) <= classes[pairs[p, 1]]
        return jnp.where(jnp.logical_and(keep_m, keep_n), factor, 0.0)

    def emit(p, m, n, block):
        block = block * weight(p, m, n)
        if m == 3:
            total[n, p] = block
        else:
            top = jnp.maximum(jnp.max(jnp.abs(block), axis=0, keepdims=True), TINY)
            outscale[m, n, pl.ds(p, 1), :] = top * (1.0 / LEVELS)
            outbox[m, n, p] = jnp.round(block * (LEVELS / top)).astype(jnp.int32).astype(jnp.int16)

    def part_copy(m, n, g):
        some = pl.ds(g * GROUP, GROUP)
        return pltpu.make_async_remote_copy(
            src_ref=outbox.at[m, n, some],
            dst_ref=inbox.at[m, n, some],
            send_sem=part_sent.at[m, n],
            recv_sem=part_got.at[m, n],
            device_id=(lax.rem(a + m + 1, 4), o),
            device_id_type=MESH,
        )

    def scale_copy(m, n):
        return pltpu.make_async_remote_copy(
            src_ref=outscale.at[m, n],
            dst_ref=inscale.at[m, n],
            send_sem=scale_sent.at[m, n],
            recv_sem=scale_got.at[m, n],
            device_id=(lax.rem(a + m + 1, 4), o),
            device_id_type=MESH,
        )

    def multiply(ms, ns):
        lo, hi = ms[0], ms[-1] + 1

        def group(g, carry):
            def one(t, carry):
                p = g * GROUP + t
                i = jnp.clip(pairs[p, 0] - start, 0, OCC_DEV - 1)
                j = jnp.clip(pairs[p, 1] - start, 0, 2 * OCC_DEV - 1)
                rows = left[i, lo * COL:hi * COL, :]
                for n in ns:
                    block = jnp.dot(rows, cols[n][j], preferred_element_type=jnp.float32)
                    for m in ms:
                        emit(p, m, n, block[(m - lo) * COL:(m - lo + 1) * COL])
                return carry

            lax.fori_loop(0, GROUP, one, 0)
            for m in ms:
                if m < 3:
                    for n in ns:
                        part_copy(m, n, g).start()
            return carry

        lax.fori_loop(0, PAIRS_DEV // GROUP, group, 0)
        for m in ms:
            if m < 3:
                for n in ns:
                    scale_copy(m, n).start()

    for q in range(4):
        arrive(q)
        settle(q)
        multiply(list(range(min(q + 1, 3))), [q])
        if 0 < q < 3:
            multiply([q], list(range(q)))
    multiply([3], [0, 1, 2, 3])

    for n in range(4):
        for m in range(3):
            wait_bytes(inbox.at[m, n], part_got.at[m, n])
            wait_bytes(inscale.at[m, n], scale_got.at[m, n])

    def finish(p, carry):
        for n in range(4):
            value = total[n, p]
            for m in range(3):
                there = (n + m + 1) % 4
                part = inbox[m, there, p].astype(jnp.int32).astype(jnp.float32)
                value = value + part * inscale[m, there, pl.ds(p, 1), :]
            out[p, :, column(n)] = value.astype(BF16)
        return carry

    lax.fori_loop(0, PAIRS_DEV, finish, 0)

    for q in range(4):
        wait_bytes(remote_part(q), sent.at[q])
    for n in range(4):
        for m in range(3):
            wait_bytes(outbox.at[m, n], part_sent.at[m, n])
            wait_bytes(outscale.at[m, n], scale_sent.at[m, n])


def on_device(slab, domain_class, pairs):
    dma = pltpu.SemaphoreType.DMA
    return pl.pallas_call(
        kernel,
        out_shape=jax.ShapeDtypeStruct((PAIRS_DEV, COL, DOM), BF16),
        in_specs=[
            pl.BlockSpec(memory_space=pltpu.SMEM),
            pl.BlockSpec(memory_space=pltpu.SMEM),
            pl.BlockSpec(memory_space=pl.ANY),
        ],
        out_specs=pl.BlockSpec(memory_space=pltpu.VMEM),
        scratch_shapes=[pltpu.VMEM((2 * OCC_DEV, KLOC, COL), BF16)] * 4 + [
            pltpu.VMEM((OCC_DEV, DOM, KLOC), BF16),
            pltpu.VMEM((4, PAIRS_DEV, COL, COL), jnp.float32),
            pltpu.VMEM((3, 4, PAIRS_DEV, COL, COL), jnp.int16),
            pltpu.VMEM((3, 4, PAIRS_DEV, COL, COL), jnp.int16),
            pltpu.VMEM((3, 4, PAIRS_DEV, COL), jnp.float32),
            pltpu.VMEM((3, 4, PAIRS_DEV, COL), jnp.float32),
            dma((4,)), dma((4,)), dma((4,)), dma((4,)), dma((4,)),
            dma((3, 4)), dma((3, 4)), dma((3, 4)), dma((3, 4)),
        ],
        compiler_params=pltpu.CompilerParams(
            collective_id=0, has_side_effects=True, vmem_limit_bytes=56 << 20
        ),
        cost_estimate=pl.CostEstimate(flops=17_000_000_000, bytes_accessed=12 << 20, transcendentals=0),
    )(domain_class, pairs, slab)


def solution(mesh):
    in_specs = (P(None, ("aux", "occ"), None), P(), P("occ", None))
    out_specs = P("occ", "aux", None)
    return jax.shard_map(
        on_device, mesh=mesh, in_specs=in_specs, out_specs=out_specs, check_vma=False
    )
```

time: 525 us -> 207 us (0.39)
  the two profiles are of different devices: /device:TPU:97 before, /device:TPU:62 now
where the time goes in v1:
time: 207 us; the launch traced here: 206 us
  Pallas kernels  202 us (98%)
  local copies, waits for them, and re-layouts  4.45 us (2%)
    pallas_call x1, Pallas kernels, on_device(): pl.pallas_call(kernel, out_shape=jax.ShapeDtypeStruct((PAIRS_DEV, COL, DO...  202 us
    unnamed x2, local copies, waits for them, and re-layouts  4.45 us

profile of v1, /device:TPU:62, one launch (start us, length us, event | category | flops | bytes accessed | tf_op | source)
XLA Modules:
  0.0 206.4 jit_solution(3548761731794680152)
XLA Ops:
  0.0 1.4 copy.4.pairs
  1.4 201.9 %shard_map.37 = bf16[16,128,512]{2,1,0:T(8,128)(2,1)} custom-call(s32[128]{0:T(128)} %classes.1, s32[16,2]{1,0:T(8,128)} %copy.4.pairs, bf16[128,64,512]{2,1,0:T(8,128)(2,1)} %slab.1), custom_call_target="tpu_custom_call" | custom-call | flops 16999999488 | bytes 12582912 | tf_op jit(solution)/shard_map/pallas_call | solution.py:247
  203.3 3.1 %copy.6 = bf16[16,128,512]{2,1,0:T(8,128)(2,1)} copy(bf16[16,128,512]{2,1,0:T(8,128)(2,1)} %shard_map.37) | data formatting | bytes 4194304

commit v2 on v1

--- a/solution.py
+++ b/solution.py
@@ -25,12 +25,14 @@
 LEVELS = 32767.0
 TINY = 1e-33
 BF16 = jnp.bfloat16
+EVENTS = tuple((part, q) for q in range(4) for part in "BAC")
+WINDOW = 5
 
 
 def kernel(classes, pairs, slab, out, *scratch):
     cols = scratch[:4]
     (left, total, outbox, inbox, outscale, inscale,
-     got, sent, own_sem, mid_got, mid_sent, part_got, part_sent, scale_got, scale_sent) = scratch[4:]
+     got, sent, kept, mid_got, mid_sent, part_got, part_sent, scale_got, scale_sent) = scratch[4:]
     a = lax.axis_index("aux")
     o = lax.axis_index("occ")
     chip = o // 2
@@ -56,72 +58,65 @@
     def column(q):
         return pl.ds(pl.multiple_of(lax.rem(a + q + 1, 4) * COL, COL), COL)
 
-    def own_copy(q, orbital, count, slot):
+    def place(part, to_chip):
+        if part == "A":
+            return 8 * to_chip, 0, 0
+        if part == "B":
+            return 8 * to_chip + 4, core, 4 - 4 * core
+        return lax.rem(8 * to_chip + 8, NOCC), 1, 4
+
+    def keep_copy(part, q):
+        orbital, _, slot = place(part, chip)
+        e = EVENTS.index((part, q))
         return pltpu.make_async_copy(
-            slab.at[pl.ds(orbital, count), :, column(q)], cols[q].at[pl.ds(slot, count), mine, :], own_sem.at[q]
-        )
-
-    def slab_copy(q, to_chip, to_core, orbital, count, slot):
+            slab.at[pl.ds(orbital, 4), :, column(q)], cols[q].at[pl.ds(slot, 4), mine, :], kept.at[e]
+        )
+
+    def slab_copy(part, q, to_chip):
+        orbital, to_core, slot = place(part, to_chip)
+        e = EVENTS.index((part, q))
         return pltpu.make_async_remote_copy(
-            src_ref=slab.at[pl.ds(orbital, count), :, column(q)],
-            dst_ref=cols[q].at[pl.ds(slot, count), mine, :],
-            send_sem=sent.at[q],
-            recv_sem=got.at[q],
+            src_ref=slab.at[pl.ds(orbital, 4), :, column(q)],
+            dst_ref=cols[q].at[pl.ds(slot, 4), mine, :],
+            send_sem=sent.at[e],
+            recv_sem=got.at[e],
             device_id=(a, 2 * to_chip + to_core),
             device_id_type=MESH,
         )
 
-    for q in range(4):
-        own_copy(q, start, OCC_DEV, 0).start()
-
-        @pl.when(core == 0)
-        def _():
-            own_copy(q, start + OCC_DEV, OCC_DEV, OCC_DEV).start()
+    for part, q in EVENTS:
+        if part == "B":
+            keep_copy(part, q).start()
+        else:
+            @pl.when(core == (part == "C"))
+            def _():
+                keep_copy(part, q).start()
 
     pl.semaphore_wait(barrier, N_OCC - 1 + N_AUX - 1)
 
-    def send_columns(q):
-        ahead = lax.rem(8 * chip + 8, NOCC)
-
-        @pl.when(core == 0)
-        def _():
-            slab_copy(q, chip, 1, ahead, 4, 4).start()
-
-        @pl.when(core == 1)
-        def _():
-            slab_copy(q, chip, 0, 8 * chip, 4, 0).start()
-            own_copy(q, ahead, 4, 4).start()
+    def send(part, q):
+        if part != "B":
+            @pl.when(core == (part == "A"))
+            def _():
+                slab_copy(part, q, chip).start()
 
         def body(s, carry):
             step = lax.rem(7 * s, CHIPS)
             step = step + core * (CHIPS - 2 * step)
             to = lax.rem(z + step // SIDE, SIDE) * SIDE + lax.rem(x + lax.rem(step, SIDE), SIDE)
-            base = 8 * to
-            beyond = lax.rem(base + 8, NOCC)
-
-            @pl.when(core == 0)
-            def _():
-                slab_copy(q, to, 0, base, 8, 0).start()
-                slab_copy(q, to, 1, beyond, 4, 4).start()
-
-            @pl.when(core == 1)
-            def _():
-                slab_copy(q, to, 0, base, 4, 0).start()
-                slab_copy(q, to, 1, base + 4, 4, 0).start()
-                slab_copy(q, to, 1, beyond, 4, 4).start()
-
+            slab_copy(part, q, to).start()
             return carry
 
         lax.fori_loop(1, CHIPS, body, 0)
 
-    for q in range(4):
-        send_columns(q)
+    for part, q in EVENTS[:WINDOW]:
+        send(part, q)
 
     def wait_bytes(ref, sem):
         pltpu.make_async_copy(ref, ref, sem).wait()
 
-    def remote_part(q):
-        return cols[q].at[:, pl.ds(0, 23 * ROWS), :]
+    def orbitals(q, sources):
+        return cols[q].at[pl.ds(0, 4), pl.ds(0, sources * ROWS), :]
 
     def middle_copy(q):
         half = pl.ds(core * HALF, HALF)
@@ -134,15 +129,28 @@
             device_id_type=MESH,
         )
 
-    def arrive(q):
-        wait_bytes(cols[q].at[:, pl.ds(0, ROWS), :], own_sem.at[q])
-        wait_bytes(remote_part(q), got.at[q])
-        middle_copy(q).start()
-
     def settle(q):
-        middle_copy(q).wait()
         for i in range(OCC_DEV):
             left[i, q * COL:(q + 1) * COL, :] = cols[q][i].T
+
+    def take(part, q):
+        e = EVENTS.index((part, q))
+        if part == "B":
+            wait_bytes(orbitals(q, 1), kept.at[e])
+            wait_bytes(orbitals(q, CHIPS - 1), got.at[e])
+            middle_copy(q).start()
+            middle_copy(q).wait()
+
+            @pl.when(core == 1)
+            def _():
+                settle(q)
+        else:
+            @pl.when(core == (part == "C"))
+            def _():
+                wait_bytes(orbitals(q, 1), kept.at[e])
+                wait_bytes(orbitals(q, N_OCC - 1), got.at[e])
+                if part == "A":
+                    settle(q)
 
     factor = 1.0 / jnp.sqrt(jnp.float32(SLAB))
 
@@ -209,13 +217,31 @@
                 for n in ns:
                     scale_copy(m, n).start()
 
-    for q in range(4):
-        arrive(q)
-        settle(q)
-        multiply(list(range(min(q + 1, 3))), [q])
-        if 0 < q < 3:
-            multiply([q], list(range(q)))
-    multiply([3], [0, 1, 2, 3])
+    here = []
+    lefts, rights = [[], []], [[], []]
+    for e, (part, q) in enumerate(EVENTS):
+        take(part, q)
+        if e + WINDOW < len(EVENTS):
+            send(*EVENTS[e + WINDOW])
+        here.append((part, q))
+        for who in range(2):
+            needs = "AB" if who == 0 else "BC"
+            old_left, old_right = lefts[who], rights[who]
+            new_left = [q] if part == needs[0] else []
+            new_right = [n for n in range(4) if n not in old_right and all((h, n) in here for h in needs)]
+            lefts[who], rights[who] = old_left + new_left, old_right + new_right
+            remote = [m for m in lefts[who] if m < 3]
+
+            @pl.when(core == who)
+            def _():
+                if new_right and remote:
+                    multiply(remote, new_right)
+                if new_left and q < 3 and old_right:
+                    multiply(new_left, old_right)
+                if 3 in old_left and new_right:
+                    multiply([3], new_right)
+                if 3 in new_left and rights[who]:
+                    multiply([3], rights[who])
 
     for n in range(4):
         for m in range(3):
@@ -234,8 +260,13 @@
 
     lax.fori_loop(0, PAIRS_DEV, finish, 0)
 
-    for q in range(4):
-        wait_bytes(remote_part(q), sent.at[q])
+    for e, (part, q) in enumerate(EVENTS):
+        wait_bytes(orbitals(q, CHIPS - 1), sent.at[e])
+        if part != "B":
+            @pl.when(core == (part == "A"))
+            def _():
+                wait_bytes(orbitals(q, 1), sent.at[e])
+
     for n in range(4):
         for m in range(3):
             wait_bytes(outbox.at[m, n], part_sent.at[m, n])
@@ -260,7 +291,7 @@
             pltpu.VMEM((3, 4, PAIRS_DEV, COL, COL), jnp.int16),
             pltpu.VMEM((3, 4, PAIRS_DEV, COL), jnp.float32),
             pltpu.VMEM((3, 4, PAIRS_DEV, COL), jnp.float32),
-            dma((4,)), dma((4,)), dma((4,)), dma((4,)), dma((4,)),
+            dma((12,)), dma((12,)), dma((12,)), dma((4,)), dma((4,)),
             dma((3, 4)), dma((3, 4)), dma((3, 4)), dma((3, 4)),
         ],
         compiler_params=pltpu.CompilerParams(

time: 207 us -> 186 us (0.90)
  the two profiles are of different devices: /device:TPU:62 before, /device:TPU:35 now
where the time goes in v2:
time: 186 us
  Pallas kernels  182 us (98%)
  local copies, waits for them, and re-layouts  4.45 us (2%)
    pallas_call x1, Pallas kernels, on_device(): pl.pallas_call(kernel, out_shape=jax.ShapeDtypeStruct((PAIRS_DEV, COL, DO...  182 us
    unnamed x2, local copies, waits for them, and re-layouts  4.45 us

profile of v2, /device:TPU:35, one launch (start us, length us, event | category | flops | bytes accessed | tf_op | source)
XLA Modules:
  0.0 186.2 jit_solution(4377855072141546669)
XLA Ops:
  0.0 1.4 copy.4.pairs
  1.4 181.8 %shard_map.37 = bf16[16,128,512]{2,1,0:T(8,128)(2,1)} custom-call(s32[128]{0:T(128)} %classes.1, s32[16,2]{1,0:T(8,128)} %copy.4.pairs, bf16[128,64,512]{2,1,0:T(8,128)(2,1)} %slab.1), custom_call_target="tpu_custom_call" | custom-call | flops 16999999488 | bytes 12582912 | tf_op jit(solution)/shard_map/pallas_call | solution.py:278
  183.2 3.1 %copy.6 = bf16[16,128,512]{2,1,0:T(8,128)(2,1)} copy(bf16[16,128,512]{2,1,0:T(8,128)(2,1)} %shard_map.37) | data formatting | bytes 4194304

commit v3 on v2

v3 whole, which is shorter than its diff:
```python
import functools

import jax
import jax.numpy as jnp
from jax import lax
from jax.experimental import pallas as pl
from jax.experimental.pallas import tpu as pltpu
from jax.sharding import PartitionSpec as P

DOM = 512
SLAB = 8192
OCC_DEV = 4
PAIRS_DEV = 16
N_AUX = 4
SIDE = 4
CHIPS = SIDE * SIDE
N_OCC = 2 * CHIPS
ROWS = 64
KLOC = N_OCC * ROWS
HALF = KLOC // 2
COL = DOM // 4
GROUP = 4
UNROLL = 4
NOCC = N_OCC * OCC_DEV
MESH = pl.DeviceIdType.MESH
LEVELS = 32767.0
TINY = 1e-33
BF16 = jnp.bfloat16
EVENTS = tuple((part, q) for part in "ABC" for q in range(4))
HELD = PAIRS_DEV // 2


def kernel(classes, pairs, slab, out, *scratch):
    cols = scratch[:4]
    (left, total, hold, outbox, inbox, outscale, inscale,
     got, sent, kept, mid_got, mid_sent, part_got, part_sent, scale_got, scale_sent) = scratch[4:]
    a = lax.axis_index("aux")
    o = lax.axis_index("occ")
    chip = o // 2
    core = lax.rem(o, 2)
    z, x = chip // SIDE, lax.rem(chip, SIDE)
    start = o * OCC_DEV
    sibling = o + 1 - 2 * core
    mine = pl.ds(core * HALF + chip * ROWS, ROWS)

    barrier = pltpu.get_barrier_semaphore()

    def greet_occ(s, carry):
        pl.semaphore_signal(barrier, inc=1, device_id=(a, lax.rem(o + s, N_OCC)), device_id_type=MESH)
        return carry

    def greet_aux(s, carry):
        pl.semaphore_signal(barrier, inc=1, device_id=(lax.rem(a + s, N_AUX), o), device_id_type=MESH)
        return carry

    lax.fori_loop(1, N_OCC, greet_occ, 0)
    greet_aux(1, 0)
    greet_aux(N_AUX - 1, 0)

    def column(q):
        return pl.ds(q * COL, COL)

    def place(part, to_chip):
        if part == "A":
            return 8 * to_chip, 0, 0
        if part == "B":
            return 8 * to_chip + 4, core, 4 - 4 * core
        return lax.rem(8 * to_chip + 8, NOCC), 1, 4

    def keep_copy(part, q):
        orbital, _, slot = place(part, chip)
        e = EVENTS.index((part, q))
        return pltpu.make_async_copy(
            slab.at[pl.ds(orbital, 4), :, column(q)], cols[q].at[pl.ds(slot, 4), mine, :], kept.at[e]
        )

    def slab_copy(part, q, to_chip):
        orbital, to_core, slot = place(part, to_chip)
        e = EVENTS.index((part, q))
        return pltpu.make_async_remote_copy(
            src_ref=slab.at[pl.ds(orbital, 4), :, column(q)],
            dst_ref=cols[q].at[pl.ds(slot, 4), mine, :],
            send_sem=sent.at[e],
            recv_sem=got.at[e],
            device_id=(a, 2 * to_chip + to_core),
            device_id_type=MESH,
        )

    for part, q in EVENTS:
        if part == "B":
            keep_copy(part, q).start()
        else:
            @pl.when(core == (part == "C"))
            def _():
                keep_copy(part, q).start()

    pl.semaphore_wait(barrier, N_OCC + 1)

    def send(part, q):
        if part != "B":
            @pl.when(core == (part == "A"))
            def _():
                slab_copy(part, q, chip).start()

        def body(s, carry):
            step = lax.rem(7 * s, CHIPS)
            step = step + core * (CHIPS - 2 * step)
            to = lax.rem(z + step // SIDE, SIDE) * SIDE + lax.rem(x + lax.rem(step, SIDE), SIDE)
            slab_copy(part, q, to).start()
            return carry

        lax.fori_loop(1, CHIPS, body, 0)

    for part, q in EVENTS:
        send(part, q)

    def wait_bytes(ref, sem):
        pltpu.make_async_copy(ref, ref, sem).wait()

    def orbitals(q, sources):
        return cols[q].at[pl.ds(0, 4), pl.ds(0, sources * ROWS), :]

    def middle_copy(q):
        half = pl.ds(core * HALF, HALF)
        return pltpu.make_async_remote_copy(
            src_ref=cols[q].at[pl.ds(4 - 4 * core, 4), half, :],
            dst_ref=cols[q].at[pl.ds(4 * core, 4), half, :],
            send_sem=mid_sent.at[q],
            recv_sem=mid_got.at[q],
            device_id=(a, sibling),
            device_id_type=MESH,
        )

    def arrived(part, q, sources):
        e = EVENTS.index((part, q))
        wait_bytes(orbitals(q, 1), kept.at[e])
        wait_bytes(orbitals(q, sources), got.at[e])

    def settle(q):
        slot = pl.multiple_of(lax.rem(q + 7 - a, 4) * COL, COL)
        for i in range(OCC_DEV):
            left[i, pl.ds(slot, COL), :] = cols[q][i].T

    factor = 1.0 / jnp.sqrt(jnp.float32(SLAB))

    def weight(p, m, n):
        keep_m = lax.rem(a + m + 1, 4) <= classes[pairs[p, 0]]
        keep_n = n <= classes[pairs[p, 1]]
        return jnp.where(jnp.logical_and(keep_m, keep_n), factor, 0.0)

    def pack(p, m, n, block):
        top = jnp.maximum(jnp.max(jnp.abs(block), axis=0, keepdims=True), TINY)
        outscale[m, n, pl.ds(p, 1), :] = top * (1.0 / LEVELS)
        outbox[m, n, p] = jnp.round(block * (LEVELS / top)).astype(jnp.int32).astype(jnp.int16)

    def unpack(p, m, n):
        return inbox[m, n, p].astype(jnp.int32).astype(jnp.float32) * inscale[m, n, pl.ds(p, 1), :]

    def toward(m, h):
        up = m == 0 or (m == 1 and h == 0)
        return lax.rem(a + (1 if up else N_AUX - 1), N_AUX), o

    def part_copy(m, n, h, g):
        some = pl.ds(g * GROUP, GROUP)
        return pltpu.make_async_remote_copy(
            src_ref=outbox.at[m, n, some],
            dst_ref=inbox.at[m, n, some],
            send_sem=part_sent.at[m, n, h],
            recv_sem=part_got.at[m, n, h],
            device_id=toward(m, h),
            device_id_type=MESH,
        )

    def half(ref, m, n, h):
        return ref.at[m, n, pl.ds(h * HELD, HELD)]

    def scale_copy(m, n, h):
        return pltpu.make_async_remote_copy(
            src_ref=half(outscale, m, n, h),
            dst_ref=half(inscale, m, n, h),
            send_sem=scale_sent.at[m, n, h],
            recv_sem=scale_got.at[m, n, h],
            device_id=toward(m, h),
            device_id_type=MESH,
        )

    def multiply(n, h):
        direct, held = (2, 0) if h == 0 else (0, 2)

        def group(g, carry):
            def one(t, carry):
                p = g * GROUP + t
                i = jnp.clip(pairs[p, 0] - start, 0, OCC_DEV - 1)
                j = jnp.clip(pairs[p, 1] - start, 0, 2 * OCC_DEV - 1)
                block = jnp.dot(left[i], cols[n][j], preferred_element_type=jnp.float32)
                for m in range(4):
                    part = block[m * COL:(m + 1) * COL] * weight(p, m, n)
                    if m == 3:
                        total[n, p] = part
                    elif m == held:
                        hold[h, n, p - h * HELD] = part
                    else:
                        pack(p, m, n, part)
                return carry

            lax.fori_loop(0, GROUP, one, 0, unroll=UNROLL)
            part_copy(1, n, h, g).start()
            part_copy(direct, n, h, g).start()
            return carry

        lax.fori_loop(h * (HELD // GROUP), (h + 1) * (HELD // GROUP), group, 0)
        scale_copy(1, n, h).start()
        scale_copy(direct, n, h).start()

    def relay(n, h):
        m = 0 if h == 0 else 2
        wait_bytes(half(inbox, 1, n, h), part_got.at[1, n, h])
        wait_bytes(half(inscale, 1, n, h), scale_got.at[1, n, h])

        def group(g, carry):
            def one(t, carry):
                p = g * GROUP + t
                pack(p, m, n, hold[h, n, p - h * HELD] + unpack(p, 1, n))
                return carry

            lax.fori_loop(0, GROUP, one, 0, unroll=UNROLL)
            part_copy(m, n, h, g).start()
            return carry

        lax.fori_loop(h * (HELD // GROUP), (h + 1) * (HELD // GROUP), group, 0)
        scale_copy(m, n, h).start()

    def finish(n, h):
        for m in (0, 2):
            wait_bytes(half(inbox, m, n, h), part_got.at[m, n, h])
            wait_bytes(half(inscale, m, n, h), scale_got.at[m, n, h])

        def one(p, carry):
            out[p, :, column(n)] = (total[n, p] + unpack(p, 0, n) + unpack(p, 2, n)).astype(BF16)
            return carry

        lax.fori_loop(h * HELD, (h + 1) * HELD, one, 0)

    @pl.when(core == 0)
    def _():
        for q in range(4):
            arrived("A", q, N_OCC - 1)
            settle(q)

    @pl.when(core == 1)
    def _():
        for q in range(4):
            arrived("B", q, CHIPS - 1)
            middle_copy(q).start()
        for q in range(4):
            middle_copy(q).wait()
            settle(q)

    for n in range(4):
        @pl.when(core == 0)
        def _():
            arrived("B", n, CHIPS - 1)
            middle_copy(n).start()
            middle_copy(n).wait()

        @pl.when(core == 1)
        def _():
            arrived("C", n, N_OCC - 1)

        multiply(n, 0)
        if n > 0:
            relay(n - 1, 0)
            relay(n - 1, 1)
        multiply(n, 1)

    relay(3, 0)
    relay(3, 1)
    for n in range(4):
        for h in range(2):
            finish(n, h)

    for e, (part, q) in enumerate(EVENTS):
        wait_bytes(orbitals(q, CHIPS - 1), sent.at[e])
        if part != "B":
            @pl.when(core == (part == "A"))
            def _():
                wait_bytes(orbitals(q, 1), sent.at[e])

    for n in range(4):
        for m in range(3):
            for h in range(2):
                wait_bytes(half(outbox, m, n, h), part_sent.at[m, n, h])
                wait_bytes(half(outscale, m, n, h), scale_sent.at[m, n, h])


def on_device(slab, domain_class, pairs):
    dma = pltpu.SemaphoreType.DMA
    return pl.pallas_call(
        kernel,
        out_shape=jax.ShapeDtypeStruct((PAIRS_DEV, COL, DOM), BF16),
        in_specs=[
            pl.BlockSpec(memory_space=pltpu.SMEM),
            pl.BlockSpec(memory_space=pltpu.SMEM),
            pl.BlockSpec(memory_space=pl.ANY),
        ],
        out_specs=pl.BlockSpec(memory_space=pltpu.VMEM),
        scratch_shapes=[pltpu.VMEM((2 * OCC_DEV, KLOC, COL), BF16)] * 4 + [
            pltpu.VMEM((OCC_DEV, DOM, KLOC), BF16),
            pltpu.VMEM((4, PAIRS_DEV, COL, COL), jnp.float32),
            pltpu.VMEM((2, 4, HELD, COL, COL), jnp.float32),
            pltpu.VMEM((3, 4, PAIRS_DEV, COL, COL), jnp.int16),
            pltpu.VMEM((3, 4, PAIRS_DEV, COL, COL), jnp.int16),
            pltpu.VMEM((3, 4, PAIRS_DEV, COL), jnp.float32),
            pltpu.VMEM((3, 4, PAIRS_DEV, COL), jnp.float32),
            dma((12,)), dma((12,)), dma((12,)), dma((4,)), dma((4,)),
            dma((3, 4, 2)), dma((3, 4, 2)), dma((3, 4, 2)), dma((3, 4, 2)),
        ],
        compiler_params=pltpu.CompilerParams(
            collective_id=0, has_side_effects=True, vmem_limit_bytes=58 << 20
        ),
        cost_estimate=pl.CostEstimate(flops=17_000_000_000, bytes_accessed=12 << 20, transcendentals=0),
    )(domain_class, pairs, slab)


def solution(mesh):
    in_specs = (P(None, ("aux", "occ"), None), P(), P("occ", None))
    out_specs = P("occ", "aux", None)
    return jax.shard_map(
        on_device, mesh=mesh, in_specs=in_specs, out_specs=out_specs, check_vma=False
    )
```

time: 186 us -> 179 us (0.962)
  the two profiles are of different devices: /device:TPU:35 before, /device:TPU:43 now
where the time goes in v3:
time: 179 us
  Pallas kernels  175 us (98%)
  local copies, waits for them, and re-layouts  4.45 us (2%)
    pallas_call x1, Pallas kernels, on_device(): pl.pallas_call(kernel, out_shape=jax.ShapeDtypeStruct((PAIRS_DEV, COL, DO...  175 us
    unnamed x2, local copies, waits for them, and re-layouts  4.45 us

profile of v3, /device:TPU:43, one launch (start us, length us, event | category | flops | bytes accessed | tf_op | source)
XLA Modules:
  0.0 179.0 jit_solution(16080795200074411094)
XLA Ops:
  0.0 1.4 copy.4.pairs
  1.4 174.5 %shard_map.37 = bf16[16,128,512]{2,1,0:T(8,128)(2,1)} custom-call(s32[128]{0:T(128)} %classes.1, s32[16,2]{1,0:T(8,128)} %copy.4.pairs, bf16[128,64,512]{2,1,0:T(8,128)(2,1)} %slab.1), custom_call_target="tpu_custom_call" | custom-call | flops 16999999488 | bytes 12582912 | tf_op jit(solution)/shard_map/pallas_call | solution.py:298
  175.9 3.1 %copy.6 = bf16[16,128,512]{2,1,0:T(8,128)(2,1)} copy(bf16[16,128,512]{2,1,0:T(8,128)(2,1)} %shard_map.37) | data formatting | bytes 4194304

commit v4 on v3

--- a/solution.py
+++ b/solution.py
@@ -28,6 +28,10 @@
 BF16 = jnp.bfloat16
 EVENTS = tuple((part, q) for part in "ABC" for q in range(4))
 HELD = PAIRS_DEV // 2
+FARTHEST = sorted(
+    [(dz, dx) for dz in range(SIDE) for dx in range(SIDE) if dz or dx],
+    key=lambda d: -sum(min(step, SIDE - step) for step in d),
+)
 
 
 def kernel(classes, pairs, slab, out, *scratch):
@@ -102,14 +106,11 @@
             def _():
                 slab_copy(part, q, chip).start()
 
-        def body(s, carry):
-            step = lax.rem(7 * s, CHIPS)
-            step = step + core * (CHIPS - 2 * step)
-            to = lax.rem(z + step // SIDE, SIDE) * SIDE + lax.rem(x + lax.rem(step, SIDE), SIDE)
+        for dz, dx in FARTHEST:
+            dz = dz + core * ((SIDE - dz) % SIDE - dz)
+            dx = dx + core * ((SIDE - dx) % SIDE - dx)
+            to = lax.rem(z + dz, SIDE) * SIDE + lax.rem(x + dx, SIDE)
             slab_copy(part, q, to).start()
-            return carry
-
-        lax.fori_loop(1, CHIPS, body, 0)
 
     for part, q in EVENTS:
         send(part, q)
@@ -144,8 +145,8 @@
     factor = 1.0 / jnp.sqrt(jnp.float32(SLAB))
 
     def weight(p, m, n):
-        keep_m = lax.rem(a + m + 1, 4) <= classes[pairs[p, 0]]
-        keep_n = n <= classes[pairs[p, 1]]
+        keep_m = lax.rem(a + m + 1, 4) <= classes[pairs[0, p]]
+        keep_n = n <= classes[pairs[1, p]]
         return jnp.where(jnp.logical_and(keep_m, keep_n), factor, 0.0)
 
     def pack(p, m, n, block):
@@ -186,14 +187,15 @@
 
     def multiply(n, h):
         direct, held = (2, 0) if h == 0 else (0, 2)
+        rows = 3 if n == 3 else 4
 
         def group(g, carry):
             def one(t, carry):
                 p = g * GROUP + t
-                i = jnp.clip(pairs[p, 0] - start, 0, OCC_DEV - 1)
-                j = jnp.clip(pairs[p, 1] - start, 0, 2 * OCC_DEV - 1)
-                block = jnp.dot(left[i], cols[n][j], preferred_element_type=jnp.float32)
-                for m in range(4):
+                i = jnp.clip(pairs[0, p] - start, 0, OCC_DEV - 1)
+                j = jnp.clip(pairs[1, p] - start, 0, 2 * OCC_DEV - 1)
+                block = jnp.dot(left[i, :rows * COL, :], cols[n][j], preferred_element_type=jnp.float32)
+                for m in range(rows):
                     part = block[m * COL:(m + 1) * COL] * weight(p, m, n)
                     if m == 3:
                         total[n, p] = part
@@ -230,6 +232,16 @@
         lax.fori_loop(h * (HELD // GROUP), (h + 1) * (HELD // GROUP), group, 0)
         scale_copy(m, n, h).start()
 
+    def multiply_own(n):
+        def one(p, carry):
+            i = jnp.clip(pairs[0, p] - start, 0, OCC_DEV - 1)
+            j = jnp.clip(pairs[1, p] - start, 0, 2 * OCC_DEV - 1)
+            part = jnp.dot(left[i, 3 * COL:, :], cols[n][j], preferred_element_type=jnp.float32)
+            total[n, p] = part * weight(p, 3, n)
+            return carry
+
+        lax.fori_loop(0, PAIRS_DEV, one, 0, unroll=UNROLL)
+
     def finish(n, h):
         for m in (0, 2):
             wait_bytes(half(inbox, m, n, h), part_got.at[m, n, h])
@@ -275,6 +287,7 @@
 
     relay(3, 0)
     relay(3, 1)
+    multiply_own(3)
     for n in range(4):
         for h in range(2):
             finish(n, h)
@@ -319,7 +332,7 @@
             collective_id=0, has_side_effects=True, vmem_limit_bytes=58 << 20
         ),
         cost_estimate=pl.CostEstimate(flops=17_000_000_000, bytes_accessed=12 << 20, transcendentals=0),
-    )(domain_class, pairs, slab)
+    )(domain_class, pairs.T, slab)
 
 
 def solution(mesh):

time: 179 us -> 175 us (0.978)
  the two profiles are of different devices: /device:TPU:43 before, /device:TPU:97 now
where the time goes in v4:
time: 175 us; the launch traced here: 174 us
  Pallas kernels  171 us (98%)
  local copies, waits for them, and re-layouts  3.1 us (2%)
    pallas_call x1, Pallas kernels, on_device(): pl.pallas_call(kernel, out_shape=jax.ShapeDtypeStruct((PAIRS_DEV, COL, DO...  171 us

profile of v4, /device:TPU:97, one launch (start us, length us, event | category | flops | bytes accessed | tf_op | source)
XLA Modules:
  0.0 174.4 jit_solution(16558187243107942760)
XLA Ops:
  0.0 171.3 %shard_map.37 = bf16[16,128,512]{2,1,0:T(8,128)(2,1)} custom-call(s32[128]{0:T(128)} %classes.1, s32[2,16]{1,0:T(2,128)} %bitcast.1, bf16[128,64,512]{2,1,0:T(8,128)(2,1)} %slab.1), custom_call_target="tpu_custom_call" | custom-call | flops 16999999488 | bytes 12582912 | tf_op jit(solution)/shard_map/pallas_call | solution.py:311
  171.3 3.1 %copy.5 = bf16[16,128,512]{2,1,0:T(8,128)(2,1)} copy(bf16[16,128,512]{2,1,0:T(8,128)(2,1)} %shard_map.37) | data formatting | bytes 4194304

commit v5 on v4

--- a/solution.py
+++ b/solution.py
@@ -306,9 +306,13 @@
                 wait_bytes(half(outscale, m, n, h), scale_sent.at[m, n, h])
 
 
+def store(sums, out):
+    out[...] = sums[...]
+
+
 def on_device(slab, domain_class, pairs):
     dma = pltpu.SemaphoreType.DMA
-    return pl.pallas_call(
+    sums = pl.pallas_call(
         kernel,
         out_shape=jax.ShapeDtypeStruct((PAIRS_DEV, COL, DOM), BF16),
         in_specs=[
@@ -333,6 +337,14 @@
         ),
         cost_estimate=pl.CostEstimate(flops=17_000_000_000, bytes_accessed=12 << 20, transcendentals=0),
     )(domain_class, pairs.T, slab)
+    block = pl.BlockSpec((PAIRS_DEV // 4, COL, DOM), lambda s: (s, 0, 0))
+    return pl.pallas_call(
+        store,
+        grid=(4,),
+        out_shape=jax.ShapeDtypeStruct((PAIRS_DEV, COL, DOM), BF16),
+        in_specs=[block],
+        out_specs=block,
+    )(sums)
 
 
 def solution(mesh):

time: 175 us -> 175 us (level)
  Pallas kernels: 171 us -> 175 us
  local copies, waits for them, and re-layouts: 3.1 us -> 0 us
    pallas_call x0 -> x1, Pallas kernels: none -> 3.78 us  [on_device(): pl.pallas_call(store, grid=(4,), out_shape=jax.ShapeDtypeStruct((PAIRS_DE...]
    unnamed x1 -> x0, local copies, waits for them, and re-layouts: 3.1 us -> none
where the time goes in v5:
time: 175 us
  Pallas kernels  175 us (100%)
    pallas_call x1, Pallas kernels, on_device(): pl.pallas_call(kernel, out_shape=jax.ShapeDtypeStruct((PAIRS_DEV, COL, DO...  171 us
    pallas_call x1, Pallas kernels, on_device(): pl.pallas_call(store, grid=(4,), out_shape=jax.ShapeDtypeStruct((PAIRS_DE...  3.78 us

profile of v5, /device:TPU:97, one launch (start us, length us, event | category | flops | bytes accessed | tf_op | source)
XLA Modules:
  0.0 175.1 jit_solution(209521786051194302)
XLA Ops:
  0.0 171.3 %shard_map.37.sums = bf16[16,128,512]{2,1,0:T(8,128)(2,1)} custom-call(s32[128]{0:T(128)} %classes.1, s32[2,16]{1,0:T(2,128)} %bitcast.1, bf16[128,64,512]{2,1,0:T(8,128)(2,1)} %slab.1), custom_call_target="tpu_custom_call" | custom-call | flops 16999999488 | bytes 12582912 | tf_op jit(solution)/shard_map/pallas_call | solution.py:315
  171.3 3.8 %shard_map.38 = bf16[16,128,512]{2,1,0:T(8,128)(2,1)} custom-call(bf16[16,128,512]{2,1,0:T(8,128)(2,1)} %shard_map.37.sums), custom_call_target="tpu_custom_call" | custom-call | tf_op jit(solution)/shard_map/pallas_call | solution.py:341
